TPU v7x, 128 devices: a whole 4x4x4 slice. The times are simulated.
128 devices in a mesh: tm: 8 (over y_lo, x), slab: 16 (over y_hi, z, core).
Axes of the slice: x: 4, y: 4 (y_hi: 2, y_lo: 2; y = y_hi * 2 + y_lo), z: 4, core: 2. Of those that a mesh axis runs over, the one named last changes fastest.
Arguments:
- u_states: bfloat16 [8, 64, 64, 8, 256], P('tm', None, 'slab'), may hold values from -6 to 6
- lam_points: float32 [8, 64, 64, 8, 256], P('tm', None, 'slab'), may hold values from -6 to 6
- weight: bfloat16 [27, 64, 64], replicated, may hold values from -0.15625 to 0.15625
- bias: float32 [64], replicated, may hold values from -3 to 3
Outputs:
- lam_new: float32 [8, 64, 64, 8, 256], P('tm', None, 'slab')
- grad_w: float32 [27, 64, 64], replicated
- grad_b: float32 [64], replicated
All inputs are finite; a program needn't handle non-finite values.
Results may differ from a plain program's by a relative error of at most 0.0065.
Values may be sent and summed in bfloat16 or wider, within the bound.
No kernel may reach another device: no remote copies, remote signals or barrier semaphores. Data moves between devices by JAX's collectives and lax.ppermute only.
A program may use at most 256 MiB of HBM per device.

v0:
```python
import functools
import math

import jax
import jax.numpy as jnp
from jax import lax
from jax.experimental import pallas as pl
from jax.experimental.pallas import tpu as pltpu
from jax.sharding import PartitionSpec as P

f32, bf16 = jnp.float32, jnp.bfloat16
STEP = 0.25


def shifts(value):
    lane = lax.broadcasted_iota(jnp.int32, value.shape, 1)
    zero = jnp.zeros((), value.dtype)
    left = jnp.where(lane == 0, zero, pltpu.roll(value, 1, 1))
    right = jnp.where(lane == 255, zero, pltpu.roll(value, 255, 1))
    return left, right


def put(wide, plane, row, pair, value):
    count = value.shape[0]
    left, right = shifts(value)
    base = pl.multiple_of(plane * 384 + row, 64)
    cols = slice(pair * 256, pair * 256 + 256)
    wide[pl.ds(base, count), cols] = left
    wide[pl.ds(base + 128, count), cols] = value
    wide[pl.ds(base + 256, count), cols] = right


def to_rows(source, z, turn):
    value = source[:, z].astype(f32).reshape(512, 256)
    turn[0] = value[:, :128]
    turn[1] = value[:, 128:]


def row_of(turn, x):
    return jnp.concatenate([turn[half, pl.ds(x, 64, stride=8), :] for half in range(2)], 1)


def pair_of(turn, pair):
    return jnp.concatenate([row_of(turn, 2 * pair), row_of(turn, 2 * pair + 1)], 0)


def products(matrix, wide, z):
    base = pl.multiple_of(z * 384, 384)
    return [
        jnp.dot(
            matrix[...],
            wide[pl.ds(base, 1152), pair * 256 : pair * 256 + 256],
            preferred_element_type=f32,
        )
        for pair in range(4)
    ]


def combined(parts, pair):
    low, high = parts[pair][0:64], parts[pair][64:128]
    if pair > 0:
        low = low + parts[pair - 1][192:256]
    if pair < 3:
        high = high + parts[pair + 1][128:192]
    return jnp.concatenate([low, high], 0)


def averaging():
    fine = lax.broadcasted_iota(jnp.int32, (256, 128), 0)
    coarse = lax.broadcasted_iota(jnp.int32, (256, 128), 1)
    return jnp.where((fine == 2 * coarse) | (fine == 2 * coarse + 1), 0.25, 0.0).astype(bf16)


def split_dot(value, matrix):
    high = value.astype(bf16)
    low = (value - high.astype(f32)).astype(bf16)
    return jnp.dot(high, matrix, preferred_element_type=f32) + jnp.dot(
        low, matrix, preferred_element_type=f32
    )


def field(planes, dtype):
    return pltpu.VMEM((planes, 128, 1024), dtype)


def widened(planes):
    return pltpu.VMEM((planes * 384, 1024), bf16)


def near(value):
    return pltpu.with_memory_space_constraint(value, pltpu.VMEM)


def run(body, name, micros, outs, ins, scratch=(), aliases=None, scalars=0, limit=8):
    in_specs = [pl.BlockSpec(memory_space=pltpu.SMEM)] * scalars
    in_specs += [pl.BlockSpec(memory_space=pltpu.VMEM)] * (len(ins) - scalars)
    return pl.pallas_call(
        body,
        out_shape=outs,
        in_specs=in_specs,
        scratch_shapes=list(scratch),
        input_output_aliases=aliases or {},
        compiler_params=pltpu.CompilerParams(vmem_limit_bytes=limit * 2**20),
        cost_estimate=pl.CostEstimate(flops=int(micros * 1e8), bytes_accessed=0, transcendentals=0),
        name=name,
    )(*ins)


TURN = pltpu.VMEM((2, 512, 128), f32)


def by_half(body):
    def kernel(half, *refs):
        for known in range(2):
            pl.when(half[0] == known)(functools.partial(body, 2 * known, *refs))

    return kernel


def own_plane(half_b, own_a, own_b, z):
    return jnp.where(half_b[0] == z // 2, own_b[z % 2], own_a[z % 2])


def open_body(half, u, out, planes, turn, arrived):
    copy = pltpu.make_async_copy(u.at[:, pl.ds(2 * half[0], 2)], planes, arrived)
    copy.start()
    copy.wait()
    for place in range(2):
        to_rows(planes, place, turn)
        for pair in range(4):
            out[place, :, pair * 256 : pair * 256 + 256] = pair_of(turn, pair).astype(bf16)


def opened(half, u):
    return pl.pallas_call(
        open_body,
        out_shape=field(2, bf16),
        in_specs=[pl.BlockSpec(memory_space=pltpu.SMEM), pl.BlockSpec(memory_space=pltpu.HBM)],
        scratch_shapes=[pltpu.VMEM((64, 2, 8, 256), bf16), TURN, pltpu.SemaphoreType.DMA(())],
        compiler_params=pltpu.CompilerParams(vmem_limit_bytes=8 * 2**20),
        cost_estimate=pl.CostEstimate(flops=10**8, bytes_accessed=0, transcendentals=0),
        name="open",
    )(half, u)


def put_plane(wide, z, value):
    for pair in range(4):
        put(wide, z, 0, pair, value[:, pair * 256 : pair * 256 + 256])


def step_state(z, matrix, offset, wide0, wide1, sens, weight):
    parts = products(matrix, wide0, z)
    base = pl.multiple_of((z + 1) * 384, 384)
    for pair in range(4):
        cols = slice(pair * 256, pair * 256 + 256)
        tanh = jnp.tanh(combined(parts, pair) + offset)
        sens[z, :, cols] = 1.0 - tanh * tanh
        value = wide0[pl.ds(base + 128, 128), cols].astype(f32) + STEP * tanh
        if weight is not None:
            value = value * weight
        put(wide1, z, 0, pair, value.astype(bf16))


def inner_body(half_b, own_a, own_b, lam, matrix, bias, wide0, wide1, sens, factor, lam_rows, average_lam, turn):
    average = averaging()
    for z in range(4):
        put_plane(wide0, z + 2, own_plane(half_b, own_a, own_b, z))
    offset = bias[...]

    def inside(z, carry):
        step_state(z, matrix, offset, wide0, wide1, sens, None)
        return carry

    lax.fori_loop(2, 4, inside, 0, unroll=True)
    def lam_plane(z, carry):
        to_rows(lam, z, turn)
        for pair in range(4):
            cols = slice(pair * 256, pair * 256 + 256)
            value = pair_of(turn, pair)
            lam_rows[z, :, cols] = value
            average_lam[z, pair] = split_dot(value[0:64] + value[64:128], average)
        return carry

    lax.fori_loop(0, 4, lam_plane, 0)


def forward_body(base, mask, wide0_in, wide1_in, sens_in, factor_in, halo, lam, matrix, bias, diag, wide0, wide1, sens, factor, cot):
    for place in range(2):
        put_plane(wide0, 3 * base + place, halo[place])
    offset = bias[...]
    for place in range(2):
        z = 2 * base + place
        step_state(z, matrix, offset, wide0, wide1, sens, mask[z])
    average = averaging()
    cot[2] = lam[base + base // 2].astype(bf16)
    for place in range(2):
        z = base + place
        parts = products(matrix, wide1, z)
        for pair in range(4):
            cols = slice(pair * 256, pair * 256 + 256)
            tanh = jnp.tanh(combined(parts, pair) + offset)
            cot[place, :, cols] = ((1.0 - tanh * tanh) * lam[z, :, cols]).astype(bf16)
            both = sens[z + 1, 0:64, cols] + sens[z + 1, 64:128, cols]
            coarse = jnp.dot(both.astype(bf16), average, preferred_element_type=f32)
            factor[z, pair] = (coarse * diag[...]).astype(bf16)


def step_back(z, matrix, wide1, wide0, middle, sens, lam, weight):
    parts = products(matrix, wide1, z)
    for pair in range(4):
        cols = slice(pair * 256, pair * 256 + 256)
        value = lam(cols) + STEP * combined(parts, pair)
        middle[z, :, cols] = value
        value = sens[z, :, cols] * value
        if weight is not None:
            value = value * weight
        put(wide0, z, 0, pair, value.astype(bf16))


def back_inner_body(half_b, own_a, own_b, lam, sens, matrix, wide1, wide0, middle, blank, blank_sums):
    for z in range(4):
        put_plane(wide1, z + 2, own_plane(half_b, own_a, own_b, z))

    def inside(z, carry):
        step_back(z, matrix, wide1, wide0, middle, sens, lambda cols: lam[z - 1, :, cols], None)
        return carry

    lax.fori_loop(2, 4, inside, 0, unroll=True)


def back_outer_body(base, mask, wide1_in, wide0_in, middle_in, halo, lam, sens, matrix, *refs):
    wide1, wide0, middle = refs[-3:]
    for place in range(2):
        put_plane(wide1, 3 * base + place, halo[place])
    z = 1 + base + base // 2
    step_back(z, matrix, wide1, wide0, middle, sens, lambda cols: lam[z - 1, :, cols], None)
    far = 2 * base + base // 2
    step_back(far, matrix, wide1, wide0, middle, sens, lambda cols: halo[2, :, cols].astype(f32), mask[far])


def back_last_body(half, wide0, middle, average_lam, factor, matrix, coarse_in, coarse):
    average = averaging()

    def last(place, carry):
        z = 2 * half[0] + place
        parts = products(matrix, wide0, z)
        for pair in range(4):
            cols = slice(pair * 256, pair * 256 + 256)
            value = middle[z + 1, :, cols] + STEP * combined(parts, pair)
            back = split_dot(value[0:64] + value[64:128], average)
            here = average_lam[z, pair]
            coarse[z, pair] = (back - here - factor[z, pair].astype(f32) * here).astype(bf16)
        return carry

    lax.fori_loop(0, 2, last, 0)


def add_plane(cot, wide, z, widened_cot, total, sums):
    zero = jnp.zeros((64, 256), bf16)
    widened_cot[0:128] = cot
    widened_cot[128:192] = jnp.concatenate([zero, cot[64:128, :768]], 1)
    widened_cot[192:256] = jnp.concatenate([cot[0:64, 256:], zero], 1)
    total[...] += lax.dot_general(
        widened_cot[...],
        wide[pl.ds(pl.multiple_of(z * 384, 384), 1152), :],
        (((1,), (1,)), ((), ())),
        preferred_element_type=f32,
    )
    for part in range(8):
        sums[...] += cot[:, part * 128 : part * 128 + 128].astype(f32)


def centre(back0, z):
    return back0[pl.ds(pl.multiple_of((z + 1) * 384 + 128, 128), 128), :]


def gradient_first_body(half_b, own_a, own_b, wide1, back0, wide0, total, sums, widened_cot):
    total[...] = jnp.zeros_like(total)
    sums[...] = jnp.zeros_like(sums)
    for z in range(4):
        add_plane(own_plane(half_b, own_a, own_b, z), wide1, z, widened_cot.at[z], total, sums)
    for index in range(3):
        z = index + 1 - half_b[0]
        add_plane(centre(back0, z), wide0, z + 1, widened_cot.at[4 + index], total, sums)


def gradient_last_body(scale, spot, back0, wide0, total_in, sums_in, total, sums, mine, others, out, widened_cot):
    z = 3 * spot[0]
    add_plane(centre(back0, z), wide0, z + 1, widened_cot, total, sums)
    lower = lax.broadcasted_iota(jnp.int32, (64, 128), 1) < 64
    for tap in range(9):
        cols = slice(tap * 128, tap * 128 + 128)
        rows = [total[64 * q : 64 * q + 64, cols] * scale for q in range(4)]
        taps = [jnp.where(lower, rows[1], rows[3]), jnp.where(lower, rows[0], rows[1]), jnp.where(lower, rows[2], rows[0])]
        taps = [value + pltpu.roll(value, 64, 1) for value in taps]
        out[tap] = jnp.where(lower, taps[0], taps[1])
        if tap % 2 == 0:
            kept = taps[2]
        else:
            out[9 + tap // 2] = jnp.where(lower, kept, taps[2])
    out[13] = kept
    out[14] = (sums[0:64] + sums[64:128]) * scale
    out[15] = jnp.zeros((64, 128), f32)
    for block in range(8):
        mine[block] = out[block + 8 * spot[0]]
        others[block] = out[block + 8 - 8 * spot[0]]


def pack_body(mine, received, coarse, factor, average_lam, out, kept):
    kept[...] = average_lam[...]
    for group in range(out.shape[0]):
        out[group, 0:128] = coarse[group]
        out[group, 128:256] = factor[group]
        out[group, 256:320] = (mine[group] + received[group]).astype(bf16)


def meet_body(mixed, out, shared):
    groups = mixed.shape[0]
    value = jnp.zeros((128, 128), f32)
    out[0] = value.astype(bf16)
    summed = mixed[0, 256:320].astype(f32)
    for group in range(groups - 1):
        value = value + mixed[group, 128:256].astype(f32) * value + mixed[group, 0:128].astype(f32)
        out[group + 1] = value.astype(bf16)
        summed = summed + mixed[group + 1, 256:320].astype(f32)
    summed = summed.astype(bf16)
    for chip in range(shared.shape[0]):
        shared[chip] = summed


def join_body(shared, carried, out):
    summed = shared[0].astype(f32)
    for chip in range(1, shared.shape[0]):
        summed = summed + shared[chip].astype(f32)
    summed = summed.astype(bf16)
    for group in range(out.shape[0]):
        out[group, 0:128] = carried[group]
        out[group, 128:192] = summed


def finish_body(lam, average_lam, joined, out, turn):
    fine = lax.broadcasted_iota(jnp.int32, (128, 256), 1)
    coarse = lax.broadcasted_iota(jnp.int32, (128, 256), 0)
    copies = jnp.where((fine == 2 * coarse) | (fine == 2 * coarse + 1), 1.0, 0.0).astype(bf16)

    def plane(z, carry):
        for pair in range(4):
            carried = joined[2 * z + pair // 2, 64 * (pair % 2) : 64 * (pair % 2) + 64]
            value = split_dot(carried.astype(f32) - average_lam[z, pair], copies)
            for half in range(2):
                for x in (2 * pair, 2 * pair + 1):
                    turn[half, pl.ds(x, 64, stride=8), :] = value[:, half * 128 : half * 128 + 128]
        added = jnp.concatenate([turn[0], turn[1]], 1).reshape(64, 8, 256)
        out[:, z] = lam[:, z] + added
        return carry

    lax.fori_loop(0, 4, plane, 0, unroll=True)


def taps_body(spot, joined, received, taps, offset):
    def block(index):
        own = joined[index % 8, 128:192].astype(f32)
        other = received[index % 8].astype(f32)
        return jnp.where(spot[0] == index // 8, own, other)

    for a in range(3):
        for c in range(3):
            tap = 3 * a + c
            both = block(tap)
            taps[9 * a + c] = both[:, :64]
            taps[9 * a + 3 + c] = both[:, 64:]
            half = 64 * (tap % 2)
            taps[9 * a + 6 + c] = block(9 + tap // 2)[:, half : half + 64]
    row = lax.broadcasted_iota(jnp.int32, (64, 64), 0)
    col = lax.broadcasted_iota(jnp.int32, (64, 64), 1)
    column = jnp.broadcast_to(jnp.sum(block(14), axis=1, keepdims=True), (64, 64))
    offset[...] = jnp.sum(jnp.where(row == col, column, 0.0), axis=0, keepdims=True)


def prepare_body(mask, weight, bias, matrix, flipped, offset, diag):
    row = lax.broadcasted_iota(jnp.int32, (64, 64), 0)
    col = lax.broadcasted_iota(jnp.int32, (64, 64), 1)
    zero = jnp.zeros((64, 64), f32)

    def column(values):
        return jnp.sum(jnp.where(row == col, values, 0.0), axis=1, keepdims=True)

    def build(out, tap):
        for a in range(3):
            for c in range(3):
                taps = [tap(9 * a + 3 * b + c) for b in range(3)]
                sides = ((taps[1], taps[2]), (taps[0], taps[1]), (taps[2], zero), (zero, taps[0]))
                start = (3 * a + c) * 128
                for place in range(4):
                    both = jnp.concatenate(sides[place], 1)
                    out[64 * place : 64 * place + 64, start : start + 128] = both.astype(bf16)

    build(matrix, lambda tap: weight[tap].astype(f32))
    build(flipped, lambda tap: weight[26 - tap].astype(f32).T)
    column_bias = jnp.broadcast_to(column(jnp.broadcast_to(bias[...], (64, 64))), (64, 256))
    offset[0:64] = column_bias
    offset[64:128] = column_bias
    diag[...] = jnp.broadcast_to(2.0 * STEP * column(weight[13].astype(f32)), (64, 128))


def beside(value):
    return lax.ppermute(value, "slab", [(i, i ^ 1) for i in range(lax.axis_size("slab"))])


def across(value):
    up = [(i, i + 1) for i in range(1, lax.axis_size("slab") - 1, 2)]
    return lax.ppermute(value, "slab", up + [(j, i) for i, j in up])


def exchanged(value, axes):
    return lax.all_to_all(value, axes, 0, 0, tiled=True)


def on_device(u_states, lam_points, weight, bias):
    u, lam = u_states[0], lam_points[0]
    slab, slabs = lax.axis_index("slab"), lax.axis_size("slab")
    groups = lax.axis_size("tm")
    ones = jnp.ones((4,), f32)
    mask = jnp.concatenate([(slab > 0).astype(f32)[None], ones, (slab < slabs - 1).astype(f32)[None]])
    spot = (slab % 2).astype(jnp.int32)[None]
    other = 1 - spot
    own_b = opened(spot, u)
    halo_b = across(own_b)
    own_a = opened(other, u)
    halo_a = beside(own_a)
    taps = pltpu.VMEM((256, 1152), bf16)
    matrix, flipped, offset, diag = run(
        prepare_body,
        "prepare",
        2,
        (taps, taps, pltpu.VMEM((128, 256), f32), pltpu.VMEM((64, 128), f32)),
        [mask, weight, bias[None]],
        scalars=1,
    )
    matrix, flipped, offset, diag = (near(v) for v in (matrix, flipped, offset, diag))
    coarse_shape = pltpu.VMEM((4, 4, 64, 128), bf16)
    average_shape = (4, 4, 64, 128)
    states = (widened(8), widened(6), field(6, f32))
    *kept, lam_rows, average_lam = run(
        inner_body,
        "inner",
        5,
        (*states, coarse_shape, field(4, f32), pltpu.VMEM(average_shape, f32)),
        [spot, near(own_a), near(own_b), lam, matrix, offset],
        [TURN],
        scalars=1,
    )

    def forward(half, kept, halo):
        return run(
            by_half(forward_body),
            "forward",
            4,
            (*states, coarse_shape, field(3, bf16)),
            [half, mask] + [near(v) for v in (*kept, halo, lam_rows)] + [matrix, offset, diag],
            aliases={2: 0, 3: 1, 4: 2, 5: 3},
            scalars=2,
        )

    *kept, own_a = forward(other, kept, halo_a)
    cot_a = beside(own_a)
    wide0, wide1, sens, factor, own_b = forward(spot, kept, halo_b)
    cot_b = across(own_b)
    scale = STEP / math.sqrt(2 * groups * slabs * 4 * 8 * 256)
    back1, back0, middle, blank, blank_sums = run(
        back_inner_body,
        "back_inner",
        3,
        (*states, coarse_shape, pltpu.VMEM((128, 128), f32)),
        [spot] + [near(v) for v in (own_a, own_b, lam_rows, sens)] + [flipped],
        scalars=1,
    )

    def back_outer(half, kept, halo, *after):
        return run(
            by_half(back_outer_body),
            "back_outer",
            3,
            states,
            [half, mask] + [near(v) for v in (*kept, halo, lam_rows, sens)] + [flipped] + [near(v) for v in after],
            aliases={2: 0, 3: 1, 4: 2},
            scalars=2,
        )

    def back_last(half, coarse):
        return run(
            back_last_body,
            "back_last",
            2,
            coarse_shape,
            [half] + [near(v) for v in (back0, middle, average_lam, factor)] + [flipped, near(coarse)],
            aliases={6: 0},
            scalars=1,
        )

    back1, back0, middle = back_outer(other, (back1, back0, middle), cot_a, blank_sums, blank)
    sums_shapes = (pltpu.VMEM((256, 1152), f32), pltpu.VMEM((128, 128), f32))
    total, sums = run(
        gradient_first_body,
        "gradient_first",
        5,
        sums_shapes,
        [spot] + [near(v) for v in (own_a, own_b, wide1, back0, wide0)],
        [pltpu.VMEM((7, 256, 1024), bf16)],
        scalars=1,
    )
    coarse = back_last(other, blank)
    back1, back0, middle = back_outer(spot, (back1, back0, middle), cot_b, sums, coarse)
    half = pltpu.VMEM((8, 64, 128), f32)
    _, _, mine, others = run(
        functools.partial(gradient_last_body, scale),
        "gradient_last",
        2,
        (*sums_shapes, half, half),
        [spot] + [near(v) for v in (back0, wide0, total, sums)],
        [pltpu.VMEM((16, 64, 128), f32), pltpu.VMEM((256, 1024), bf16)],
        aliases={3: 0, 4: 1},
        scalars=1,
    )
    received = beside(others)
    coarse = back_last(spot, coarse)
    pieces = (groups, 128, 128)
    mixed, average_lam = run(
        pack_body,
        "pack",
        1,
        (jax.ShapeDtypeStruct((groups, 320, 128), bf16), jax.ShapeDtypeStruct(average_shape, f32)),
        [near(v) for v in (mine, received, coarse.reshape(pieces), factor.reshape(pieces), average_lam)],
    )
    carried, shared = run(
        meet_body,
        "meet",
        1,
        (jax.ShapeDtypeStruct(pieces, bf16), jax.ShapeDtypeStruct((slabs // 2, 64, 128), bf16)),
        [exchanged(mixed, "tm")],
    )
    same_core = [list(range(core, slabs, 2)) for core in range(2)]
    shared = lax.all_to_all(shared, "slab", 0, 0, tiled=True, axis_index_groups=same_core)
    joined = run(
        join_body,
        "join",
        1,
        jax.ShapeDtypeStruct((groups, 192, 128), bf16),
        [shared, carried],
    )
    joined = exchanged(joined, "tm")
    received = beside(joined[:, 128:])
    updated = run(
        finish_body,
        "finish",
        3,
        jax.ShapeDtypeStruct(lam.shape, f32),
        [lam, average_lam, joined],
        [TURN],
    )
    taps, offset = run(
        taps_body,
        "taps",
        1,
        (jax.ShapeDtypeStruct(weight.shape, f32), jax.ShapeDtypeStruct((1, 64), f32)),
        [spot, joined, received],
        scalars=1,
    )
    return updated[None], taps, offset[0]


def solution(mesh):
    in_specs = (P("tm", None, "slab", None, None), P("tm", None, "slab", None, None), P(), P())
    out_specs = (P("tm", None, "slab", None, None), P(), P())
    return jax.shard_map(
        on_device, mesh=mesh, in_specs=in_specs, out_specs=out_specs, check_vma=False
    )
```

profile of v0, /device:TPU:1, one launch (start us, length us, event | category | flops | bytes accessed | tf_op | source)
XLA Modules:
  0.0 93.0 jit_solution(14466364995811887680)
XLA Ops:
  0.6 0.0 copy-start
  0.7 0.0 copy-start.1
  0.7 1.4 %copy-done.1 = bf16[1,64,4,8,256]{4,3,2,1,0:T(8,128)(2,1)S(1)} copy-done((bf16[1,64,4,8,256]{4,3,2,1,0:T(8,128)(2,1)S(1)}, bf16[1,64,4,8,256]{4,3,2,1,0:T(8,128)(2,1)}, u32[]{:S(2)}) %copy-start.1) | copy-done | bytes 1048600
  2.0 0.3 open.2.own_a
  2.4 1.5 %collective-permute-start = (bf16[2,128,1024]{2,1,0:T(8,128)(2,1)S(1)}, bf16[2,128,1024]{2,1,0:T(8,128)(2,1)}, u32[]{:S(2)}, u32[]{:S(2)}) collective-permute-start(bf16[2,128,1024]{2,1,0:T(8,128)(2,1)S(1)} %open.2.own_a), channel_id=1, source_target_pairs={{0,1},{1,0},{2,3},{3,2},{4,5},{5,4},{6,7},{7,6},{8,9},{9,8},{10,11... | collective-permute-start | bytes 1572872 | tf_op jit(solution)/shard_map/ppermute | solution.py:407
  3.9 0.0 copy-start.2
  3.9 1.2 %copy-done.2 = bf16[1,64,4,8,256]{4,3,2,1,0:T(8,128)(2,1)S(1)} copy-done((bf16[1,64,4,8,256]{4,3,2,1,0:T(8,128)(2,1)S(1)}, bf16[1,64,4,8,256]{4,3,2,1,0:T(8,128)(2,1)}, u32[]{:S(2)}) %copy-start.2) | copy-done | bytes 1048600
  5.1 0.3 open.3.own_b
  5.4 3.5 %collective-permute-start.1 = (bf16[2,128,1024]{2,1,0:T(8,128)(2,1)S(1)}, bf16[2,128,1024]{2,1,0:T(8,128)(2,1)}, u32[]{:S(2)}, u32[]{:S(2)}) collective-permute-start(bf16[2,128,1024]{2,1,0:T(8,128)(2,1)S(1)} %open.3.own_b), channel_id=1, source_target_pairs={{1,2},{3,4},{5,6},{7,8},{9,10},{11,12},{13,14},{2,1},{4,3},{6,5},{... | collective-permute-start | bytes 1572872 | tf_op jit(solution)/shard_map/ppermute | solution.py:412
  9.0 0.1 pad_maximum_fusion.mask.refs_0_
  9.0 0.0 copy-start.3
  9.1 1.0 %copy-done.3 = bf16[27,64,64]{2,1,0:T(8,128)(2,1)S(1)} copy-done((bf16[27,64,64]{2,1,0:T(8,128)(2,1)S(1)}, bf16[27,64,64]{2,1,0:T(8,128)(2,1)}, u32[]{:S(2)}) %copy-start.3) | copy-done | bytes 221208
  10.1 0.0 copy-start.4
  10.1 0.7 copy-done.4
  10.7 1.1 %prepare.1 = (bf16[256,1152]{1,0:T(8,128)(2,1)S(1)}, bf16[256,1152]{1,0:T(8,128)(2,1)S(1)}, f32[128,256]{1,0:T(8,128)S(1)}, f32[64,128]{1,0:T(8,128)S(1)}) custom-call(f32[6]{0:T(128)S(1)} %pad_maximum_fusion.mask.refs_0_, bf16[27,64,64]{2,1,0:T(8,128)(2,1)S(1)} %copy-done.3, f32[1,64]{1,0:T(1,128)S(1)} %bitcast.16), custom_call_target="tpu_custom_call" | custom-call | flops 200000000 | tf_op jit(solution)/shard_map/prepare/pallas_call | solution.py:97
  11.8 0.0 copy-done
  11.8 3.1 %inner.1 = (bf16[3072,1024]{1,0:T(8,128)(2,1)S(1)}, bf16[2304,1024]{1,0:T(8,128)(2,1)S(1)}, f32[6,128,1024]{2,1,0:T(8,128)S(1)}, bf16[4,4,64,128]{3,2,1,0:T(8,12...) custom-call(s32[1]{0:T(128)} %bitcast.1.half.half_b.spot, bf16[2,128,1024]{2,1,0:T(8,128)(2,1)S(1)} %open.2.own_a, ...), custom_call_target="tpu_custom_call" | custom-call | flops 500000000 | tf_op jit(solution)/shard_map/inner/pallas_call | solution.py:97
  14.9 0.0 collective-permute-done.refs_5_
  14.9 4.4 %forward.2 = (bf16[3072,1024]{1,0:T(8,128)(2,1)S(1)}, bf16[2304,1024]{1,0:T(8,128)(2,1)S(1)}, f32[6,128,1024]{2,1,0:T(8,128)S(1)}, bf16[4,4,64,128]{3,2,1,0:T(8,128)(2,1)S(1)}, bf16[3,128,1024]{2,1,0:T(8,128)(2,1)S(1)}) custom-call(s32[1]{0:T(128)S(6)} %sub.3.half, ...), custom_call_target="tpu_custom_call", output_to_operand_aliasing={{0}: (2, {}), {1}: (3, {}), {2}: (4, {}), {3}: (5, {})} | custom-call | flops 400000000 | tf_op jit(solution)/shard_map/forward/pallas_call | solution.py:97
  19.3 0.1 collective-permute-start.2
  19.4 0.0 collective-permute-done.1.refs_5_
  19.4 4.5 %forward.3 = (bf16[3072,1024]{1,0:T(8,128)(2,1)S(1)}, bf16[2304,1024]{1,0:T(8,128)(2,1)S(1)}, f32[6,128,1024]{2,1,0:T(8,128)S(1)}, bf16[4,4,64,128]{3,2,1,0:T(8,128)(2,1)S(1)}, bf16[3,128,1024]{2,1,0:T(8,128)(2,1)S(1)}) custom-call(s32[1]{0:T(128)} %bitcast.1.half.half_b.spot, ...), custom_call_target="tpu_custom_call", output_to_operand_aliasing={{0}: (2, {}), {1}: (3, {}), {2}: (4, {}), {3}: (5, {})} | custom-call | flops 400000000 | tf_op jit(solution)/shard_map/forward/pallas_call | solution.py:97
  23.9 4.0 %collective-permute-start.3 = (bf16[3,128,1024]{2,1,0:T(8,128)(2,1)S(1)}, bf16[3,128,1024]{2,1,0:T(8,128)(2,1)S(1)}, u32[]{:S(2)}, u32[]{:S(2)}) collective-permute-start(bf16[3,128,1024]{2,1,0:T(8,128)(2,1)S(1)} %get-tuple-element.56.own_b), channel_id=1, source_target_pairs={{1,2},{3,4},{5,6},{7,8},{9,10},{11,12},{13,14},{2,1},{4,3},{6,5},{... | collective-permute-start | bytes 2359304 | tf_op jit(solution)/shard_map/ppermute | solution.py:412
  27.9 1.8 %back_inner.1 = (bf16[3072,1024]{1,0:T(8,128)(2,1)S(1)}, bf16[2304,1024]{1,0:T(8,128)(2,1)S(1)}, f32[6,128,1024]{2,1,0:T(8,128)S(1)}, bf16[4,4,64,128]{3,2,1,0:T(8,128)(2,1)S(1)}, f32[128,128]{1,0:T(8,128)S(1)}) custom-call(s32[1]{0:T(128)} %bitcast.1.half.half_b.spot, bf16[3,128,1024]{2,1,0:T(8,128)(2,1)S(1)} %get-tuple-element.51.own_a, ...), custom_call_target="tpu_custom_call" | custom-call | flops 300000000 | tf_op jit(solution)/shard_map/back_inner/pallas_call | solution.py:97
  29.7 0.0 collective-permute-done.2.refs_4_
  29.8 2.6 %back_outer.2 = (bf16[3072,1024]{1,0:T(8,128)(2,1)S(1)}, bf16[2304,1024]{1,0:T(8,128)(2,1)S(1)}, f32[6,128,1024]{2,1,0:T(8,128)S(1)}) custom-call(s32[1]{0:T(128)S(6)} %sub.3.half, f32[6]{0:T(128)S(1)} %pad_maximum_fusion.mask.refs_0_, bf16[3072,1024]{1,0:T(8,128)(2,1)S(1)} %get-tuple-element.59.refs_1_, ...), custom_call_target="tpu_custom_call", output_to_operand_aliasing={{0}: (2, {}), {1}: (3, {}), {2}: (4, {})} | custom-call | flops 300000000 | tf_op jit(solution)/shard_map/back_outer/pallas_call | solution.py:97
  32.3 2.2 %back_last.2.refs_9_.coarse_in = bf16[4,4,64,128]{3,2,1,0:T(8,128)(2,1)S(1)} custom-call(s32[1]{0:T(128)S(6)} %sub.3.half, bf16[2304,1024]{1,0:T(8,128)(2,1)S(1)} %get-tuple-element.65.back0.wide0.refs_2_, f32[6,128,1024]{2,1,0:T(8,128)S(1)} %get-tuple-element.66.middle.refs_3_, ...), custom_call_target="tpu_custom_call", output_to_operand_aliasing={{}: (6, {})} | custom-call | flops 200000000 | tf_op jit(solution)/shard_map/back_last/pallas_call | solution.py:97
  34.5 5.0 %gradient_first.1 = (f32[256,1152]{1,0:T(8,128)S(1)}, f32[128,128]{1,0:T(8,128)S(1)}) custom-call(s32[1]{0:T(128)} %bitcast.1.half.half_b.spot, bf16[3,128,1024]{2,1,0:T(8,128)(2,1)S(1)} %get-tuple-element.51.own_a, bf16[3,128,1024]{2,1,0:T(8,128)(2,1)S(1)} %get-tuple-element.56.own_b, bf16[2304,1024]{1,0:T(8,128)(2,1)S(1)} %get-tuple-element.67.wide1, ...), custom_call_target="tpu_custom_call" | custom-call | flops 500000000 | tf_op jit(solution)/shard_map/gradient_first/pallas_call | solution.py:97
  39.5 0.0 collective-permute-done.3.refs_4_
  39.5 2.3 %back_outer.3 = (bf16[3072,1024]{1,0:T(8,128)(2,1)S(1)}, bf16[2304,1024]{1,0:T(8,128)(2,1)S(1)}, f32[6,128,1024]{2,1,0:T(8,128)S(1)}) custom-call(s32[1]{0:T(128)} %bitcast.1.half.half_b.spot, f32[6]{0:T(128)S(1)} %pad_maximum_fusion.mask.refs_0_, ...), custom_call_target="tpu_custom_call", output_to_operand_aliasing={{0}: (2, {}), {1}: (3, {}), {2}: (4, {})} | custom-call | flops 300000000 | tf_op jit(solution)/shard_map/back_outer/pallas_call | solution.py:97
  41.8 1.1 %gradient_last.1 = (f32[256,1152]{1,0:T(8,128)S(1)}, f32[128,128]{1,0:T(8,128)S(1)}, f32[8,64,128]{2,1,0:T(8,128)S(1)}, f32[8,64,128]{2,1,0:T(8,128)S(1)}) custom-call(s32[1]{0:T(128)} %bitcast.1.half.half_b.spot, bf16[2304,1024]{1,0:T(8,128)(2,1)S(1)} %get-tuple-element.72.back0.wide0, ...), custom_call_target="tpu_custom_call", output_to_operand_aliasing={{0}: (3, {}), {1}: (4, {})} | custom-call | flops 200000000 | tf_op jit(solution)/shard_map/gradient_last/pallas_call | solution.py:97
  42.9 0.1 collective-permute-start.4
  43.0 2.2 %back_last.3 = bf16[4,4,64,128]{3,2,1,0:T(8,128)(2,1)S(1)} custom-call(s32[1]{0:T(128)} %bitcast.1.half.half_b.spot, bf16[2304,1024]{1,0:T(8,128)(2,1)S(1)} %get-tuple-element.72.back0.wide0, f32[6,128,1024]{2,1,0:T(8,128)S(1)} %get-tuple-element.76.middle, f32[4,4,64,128]{3,2,1,0:T(8,128)S(1)} %get-tuple-element.70.average_lam, ...), custom_call_target="tpu_custom_call", output_to_operand_aliasing={{}: (6, {})} | custom-call | flops 200000000 | tf_op jit(solution)/shard_map/back_last/pallas_call | solution.py:97
  45.2 0.0 collective-permute-done.4.received
  45.2 0.1 pack.1
  45.3 16.0 %all_to_all.15.mixed = bf16[8,320,128]{2,1,0:T(8,128)(2,1)S(1)} all-to-all(bf16[8,320,128]{2,1,0:T(8,128)(2,1)S(1)} %get-tuple-element.78), channel_id=1, replica_groups=mesh['tm'=8,'slab'=16] {'tm'}, dimensions={0} | all-to-all | bytes 1310720 | tf_op jit(solution)/shard_map/all_to_all | solution.py:416
  61.3 0.1 meet.1
  61.4 15.5 %all_to_all.16.shared = bf16[8,64,128]{2,1,0:T(8,128)(2,1)S(1)} all-to-all(bf16[8,64,128]{2,1,0:T(8,128)(2,1)S(1)} %get-tuple-element.79), channel_id=1, replica_groups={{0,2,4,6,8,10,12,14},{1,3,5,7,9,11,13,15},{16,18,20,22,24,26,28,30},{17..., dimensions={0} | all-to-all | bytes 262144 | tf_op jit(solution)/shard_map/all_to_all | solution.py:543
  76.9 9.3 %all_to_all.17.joined = bf16[8,192,128]{2,1,0:T(8,128)(2,1)S(1)} all-to-all(bf16[8,192,128]{2,1,0:T(8,128)(2,1)S(1)} %join.1), channel_id=1, replica_groups=mesh['tm'=8,'slab'=16] {'tm'}, dimensions={0} | all-to-all | bytes 786432 | tf_op jit(solution)/shard_map/all_to_all | solution.py:416
  86.2 3.7 %collective-permute-start.5 = (bf16[8,64,128]{2,1,0:T(8,128)(2,1)S(1)}, bf16[8,64,128]{2,1,0:T(8,128)(2,1)S(1)}, u32[]{:S(2)}, u32[]{:S(2)}) collective-permute-start(bf16[8,64,128]{2,1,0:T(8,128)(2,1)S(1)} %slice.4), channel_id=1, source_target_pairs={{0,1},{1,0},{2,3},{3,2},{4,5},{5,4},{6,7},{7,6},{8,9},{9,8},{10,11... | collective-permute-start | bytes 393224 | tf_op jit(solution)/shard_map/ppermute | solution.py:407
  89.9 2.1 %finish.1 = f32[64,4,8,256]{3,2,1,0:T(8,128)} custom-call(f32[64,4,8,256]{3,2,1,0:T(8,128)S(1)} %bitcast.11, f32[4,4,64,128]{3,2,1,0:T(8,128)S(1)} %get-tuple-element.77.average_lam, bf16[8,192,128]{2,1,0:T(8,128)(2,1)S(1)} %all_to_all.17.joined), custom_call_target="tpu_custom_call" | custom-call | flops 300000000 | tf_op jit(solution)/shard_map/finish/pallas_call | solution.py:97
  92.0 0.0 collective-permute-done.5.received
  92.0 1.1 %taps.1 = (f32[27,64,64]{2,1,0:T(8,128)}, f32[1,64]{1,0:T(1,128)}) custom-call(s32[1]{0:T(128)} %bitcast.1.half.half_b.spot, bf16[8,192,128]{2,1,0:T(8,128)(2,1)S(1)} %all_to_all.17.joined, bf16[8,64,128]{2,1,0:T(8,128)(2,1)S(1)} %collective-permute-done.5.received), custom_call_target="tpu_custom_call" | custom-call | flops 100000000 | tf_op jit(solution)/shard_map/taps/pallas_call | solution.py:97
  (3 shorter events, 0.0 us)
Async XLA Ops:
  0.6 11.2 %copy-start = (f32[1,64,4,8,256]{4,3,2,1,0:T(8,128)S(1)}, f32[1,64,4,8,256]{4,3,2,1,0:T(8,128)}, u32[]{:S(2)}) copy-start(f32[1,64,4,8,256]{4,3,2,1,0:T(8,128)} %param.5) | copy-start | bytes 6291460
  0.7 1.4 %copy-start.1 = (bf16[1,64,4,8,256]{4,3,2,1,0:T(8,128)(2,1)S(1)}, bf16[1,64,4,8,256]{4,3,2,1,0:T(8,128)(2,1)}, u32[]{:S(2)}) copy-start(bf16[1,64,4,8,256]{4,3,2,1,0:T(8,128)(2,1)} %param.4) | copy-start | bytes 3145732
  2.4 12.6 %collective-permute-start = (bf16[2,128,1024]{2,1,0:T(8,128)(2,1)S(1)}, bf16[2,128,1024]{2,1,0:T(8,128)(2,1)}, u32[]{:S(2)}, u32[]{:S(2)}) collective-permute-start(bf16[2,128,1024]{2,1,0:T(8,128)(2,1)S(1)} %open.2.own_a), channel_id=1, source_target_pairs={{0,1},{1,0},{2,3},{3,2},{4,5},{5,4},{6,7},{7,6},{8,9},{9,8},{10,11... | collective-permute-start | bytes 1572872 | tf_op jit(solution)/shard_map/ppermute | solution.py:407
  3.9 1.2 %copy-start.2 = (bf16[1,64,4,8,256]{4,3,2,1,0:T(8,128)(2,1)S(1)}, bf16[1,64,4,8,256]{4,3,2,1,0:T(8,128)(2,1)}, u32[]{:S(2)}) copy-start(bf16[1,64,4,8,256]{4,3,2,1,0:T(8,128)(2,1)} %param.4) | copy-start | bytes 3145732
  5.4 14.0 %collective-permute-start.1 = (bf16[2,128,1024]{2,1,0:T(8,128)(2,1)S(1)}, bf16[2,128,1024]{2,1,0:T(8,128)(2,1)}, u32[]{:S(2)}, u32[]{:S(2)}) collective-permute-start(bf16[2,128,1024]{2,1,0:T(8,128)(2,1)S(1)} %open.3.own_b), channel_id=1, source_target_pairs={{1,2},{3,4},{5,6},{7,8},{9,10},{11,12},{13,14},{2,1},{4,3},{6,5},{... | collective-permute-start | bytes 1572872 | tf_op jit(solution)/shard_map/ppermute | solution.py:412
  9.0 1.0 %copy-start.3 = (bf16[27,64,64]{2,1,0:T(8,128)(2,1)S(1)}, bf16[27,64,64]{2,1,0:T(8,128)(2,1)}, u32[]{:S(2)}) copy-start(bf16[27,64,64]{2,1,0:T(8,128)(2,1)} %weight.1) | copy-start | bytes 663556
  10.1 0.7 copy-start.4
  19.3 10.4 %collective-permute-start.2 = (bf16[3,128,1024]{2,1,0:T(8,128)(2,1)S(1)}, bf16[3,128,1024]{2,1,0:T(8,128)(2,1)S(1)}, u32[]{:S(2)}, u32[]{:S(2)}) collective-permute-start(bf16[3,128,1024]{2,1,0:T(8,128)(2,1)S(1)} %get-tuple-element.51.own_a), channel_id=1, source_target_pairs={{0,1},{1,0},{2,3},{3,2},{4,5},{5,4},{6,7},{7,6},{8,9},{9,8},{10,11... | collective-permute-start | bytes 2359304 | tf_op jit(solution)/shard_map/ppermute | solution.py:407
  23.9 15.6 %collective-permute-start.3 = (bf16[3,128,1024]{2,1,0:T(8,128)(2,1)S(1)}, bf16[3,128,1024]{2,1,0:T(8,128)(2,1)S(1)}, u32[]{:S(2)}, u32[]{:S(2)}) collective-permute-start(bf16[3,128,1024]{2,1,0:T(8,128)(2,1)S(1)} %get-tuple-element.56.own_b), channel_id=1, source_target_pairs={{1,2},{3,4},{5,6},{7,8},{9,10},{11,12},{13,14},{2,1},{4,3},{6,5},{... | collective-permute-start | bytes 2359304 | tf_op jit(solution)/shard_map/ppermute | solution.py:412
  42.9 2.3 %collective-permute-start.4 = (f32[8,64,128]{2,1,0:T(8,128)S(1)}, f32[8,64,128]{2,1,0:T(8,128)S(1)}, u32[]{:S(2)}, u32[]{:S(2)}) collective-permute-start(f32[8,64,128]{2,1,0:T(8,128)S(1)} %get-tuple-element.75), channel_id=1, source_target_pairs={{0,1},{1,0},{2,3},{3,2},{4,5},{5,4},{6,7},{7,6},{8,9},{9,8},{10,11... | collective-permute-start | bytes 786440 | tf_op jit(solution)/shard_map/ppermute | solution.py:407
  86.2 5.8 %collective-permute-start.5 = (bf16[8,64,128]{2,1,0:T(8,128)(2,1)S(1)}, bf16[8,64,128]{2,1,0:T(8,128)(2,1)S(1)}, u32[]{:S(2)}, u32[]{:S(2)}) collective-permute-start(bf16[8,64,128]{2,1,0:T(8,128)(2,1)S(1)} %slice.4), channel_id=1, source_target_pairs={{0,1},{1,0},{2,3},{3,2},{4,5},{5,4},{6,7},{7,6},{8,9},{9,8},{10,11... | collective-permute-start | bytes 393224 | tf_op jit(solution)/shard_map/ppermute | solution.py:407
where the time goes:
time: 93.5 us; the launch traced here: 93 us
  blocking collectives  40.7 us (44%)
  Pallas kernels  34.2 us (37%)
  starting transfers between devices  12.9 us (14%)
  local copies, waits for them, and re-layouts  4.28 us (5%)
    pallas_call x16, Pallas kernels, run(): pl.pallas_call(body, out_shape=outs, in_specs=in_specs, scratch_shapes=li...  33.6 us
    all_to_all x2, blocking collectives, exchanged(): return lax.all_to_all(value, axes, 0, 0, tiled=True)  25.2 us
    all_to_all x1, blocking collectives, on_device(): lax.all_to_all(shared, 'slab', 0, 0, tiled=True, axis_index_groups=same_c...  15.5 us
    ppermute x2, starting transfers between devices, across(): return lax.ppermute(value, 'slab', up + [(j, i) for i, j in up])  7.5 us
    ppermute x4, starting transfers between devices, beside(): lax.ppermute(value, 'slab', [(i, i ^ 1) for i in range(lax.axis_size('sla...  5.42 us
    unnamed x10, local copies, waits for them, and re-layouts  4.26 us
  transfers between devices with their start and end apart: 6, of which 0 were waited for; matrix products, arithmetic and copies ran while one was open for 0% of the time, Pallas kernels for 31%

commit v1 on v0

--- a/solution.py
+++ b/solution.py
@@ -121,7 +121,8 @@
     return jnp.where(half_b[0] == z // 2, own_b[z % 2], own_a[z % 2])
 
 
-def open_body(half, u, out, planes, turn, arrived):
+def open_body(half, u, *refs):
+    out, planes, turn, arrived = refs[-4:]
     copy = pltpu.make_async_copy(u.at[:, pl.ds(2 * half[0], 2)], planes, arrived)
     copy.start()
     copy.wait()
@@ -131,16 +132,16 @@
             out[place, :, pair * 256 : pair * 256 + 256] = pair_of(turn, pair).astype(bf16)
 
 
-def opened(half, u):
+def opened(half, u, *after):
     return pl.pallas_call(
         open_body,
         out_shape=field(2, bf16),
-        in_specs=[pl.BlockSpec(memory_space=pltpu.SMEM), pl.BlockSpec(memory_space=pltpu.HBM)],
+        in_specs=[pl.BlockSpec(memory_space=pltpu.SMEM)] + [pl.BlockSpec(memory_space=pl.ANY)] * (1 + len(after)),
         scratch_shapes=[pltpu.VMEM((64, 2, 8, 256), bf16), TURN, pltpu.SemaphoreType.DMA(())],
         compiler_params=pltpu.CompilerParams(vmem_limit_bytes=8 * 2**20),
         cost_estimate=pl.CostEstimate(flops=10**8, bytes_accessed=0, transcendentals=0),
         name="open",
-    )(half, u)
+    )(half, pltpu.with_memory_space_constraint(u, pltpu.HBM), *after)
 
 
 def put_plane(wide, z, value):
@@ -181,7 +182,7 @@
             average_lam[z, pair] = split_dot(value[0:64] + value[64:128], average)
         return carry
 
-    lax.fori_loop(0, 4, lam_plane, 0)
+    lax.fori_loop(0, 4, lam_plane, 0, unroll=True)
 
 
 def forward_body(base, mask, wide0_in, wide1_in, sens_in, factor_in, halo, lam, matrix, bias, diag, wide0, wide1, sens, factor, cot):
@@ -377,7 +378,15 @@
     offset[...] = jnp.sum(jnp.where(row == col, column, 0.0), axis=0, keepdims=True)
 
 
-def prepare_body(mask, weight, bias, matrix, flipped, offset, diag):
+def prepare_body(mask, weight_in, bias_in, matrix, flipped, offset, diag, weight, bias, arrived):
+    copies = [
+        pltpu.make_async_copy(source, target, arrived.at[index])
+        for index, (source, target) in enumerate(((weight_in, weight), (bias_in, bias)))
+    ]
+    for copy in copies:
+        copy.start()
+    for copy in copies:
+        copy.wait()
     row = lax.broadcasted_iota(jnp.int32, (64, 64), 0)
     col = lax.broadcasted_iota(jnp.int32, (64, 64), 1)
     zero = jnp.zeros((64, 64), f32)
@@ -426,17 +435,22 @@
     other = 1 - spot
     own_b = opened(spot, u)
     halo_b = across(own_b)
-    own_a = opened(other, u)
+    own_a = opened(other, u, own_b)
     halo_a = beside(own_a)
     taps = pltpu.VMEM((256, 1152), bf16)
-    matrix, flipped, offset, diag = run(
+    matrix, flipped, offset, diag = pl.pallas_call(
         prepare_body,
-        "prepare",
-        2,
-        (taps, taps, pltpu.VMEM((128, 256), f32), pltpu.VMEM((64, 128), f32)),
-        [mask, weight, bias[None]],
-        scalars=1,
-    )
+        out_shape=(taps, taps, pltpu.VMEM((128, 256), f32), pltpu.VMEM((64, 128), f32)),
+        in_specs=[pl.BlockSpec(memory_space=pltpu.SMEM)] + [pl.BlockSpec(memory_space=pl.ANY)] * 2,
+        scratch_shapes=[
+            pltpu.VMEM(weight.shape, bf16),
+            pltpu.VMEM((1, 64), f32),
+            pltpu.SemaphoreType.DMA((2,)),
+        ],
+        compiler_params=pltpu.CompilerParams(vmem_limit_bytes=8 * 2**20),
+        cost_estimate=pl.CostEstimate(flops=10**8, bytes_accessed=0, transcendentals=0),
+        name="prepare",
+    )(mask, *(pltpu.with_memory_space_constraint(v, pltpu.HBM) for v in (weight, bias[None])))
     matrix, flipped, offset, diag = (near(v) for v in (matrix, flipped, offset, diag))
     coarse_shape = pltpu.VMEM((4, 4, 64, 128), bf16)
     average_shape = (4, 4, 64, 128)

time: 93.5 us -> 91.7 us (0.981)
  local copies, waits for them, and re-layouts: 4.28 us -> 0.02 us
  Pallas kernels: 34.2 us -> 36.8 us
    unnamed x10 -> x2, local copies, waits for them, and re-layouts: 4.26 us -> 0.01 us
    pallas_call x2, Pallas kernels: 0.64 us -> 2.73 us  [opened(): pl.pallas_call(open_body, out_shape=field(2, bf16), in_specs=[pl.BlockSpe...]
    pallas_call x0 -> x1, Pallas kernels: none -> 2.09 us  [on_device(): pl.pallas_call(prepare_body, out_shape=(taps, taps, pltpu.VMEM((128, 256)...]
    pallas_call x16 -> x15, Pallas kernels: 33.6 us -> 32 us  [run(): pl.pallas_call(body, out_shape=outs, in_specs=in_specs, scratch_shapes=li...]
  transfers between devices with their start and end apart: 6 -> 6, of which waited for: 0 -> 0; matrix products, arithmetic and copies ran while one was open for 0% -> 0% of each run, Pallas kernels for 31% -> 32%
where the time goes in v1:
time: 91.7 us; the launch traced here: 91.3 us
  blocking collectives  40.7 us (44%)
  Pallas kernels  36.8 us (40%)
  starting transfers between devices  12.9 us (14%)
    pallas_call x15, Pallas kernels, run(): pl.pallas_call(body, out_shape=outs, in_specs=in_specs, scratch_shapes=li...  32 us
    all_to_all x2, blocking collectives, exchanged(): return lax.all_to_all(value, axes, 0, 0, tiled=True)  25.2 us
    all_to_all x1, blocking collectives, on_device(): lax.all_to_all(shared, 'slab', 0, 0, tiled=True, axis_index_groups=same_c...  15.4 us
    ppermute x2, starting transfers between devices, across(): return lax.ppermute(value, 'slab', up + [(j, i) for i, j in up])  7.48 us
    ppermute x4, starting transfers between devices, beside(): lax.ppermute(value, 'slab', [(i, i ^ 1) for i in range(lax.axis_size('sla...  5.42 us
    pallas_call x2, Pallas kernels, opened(): pl.pallas_call(open_body, out_shape=field(2, bf16), in_specs=[pl.BlockSpe...  2.73 us
    pallas_call x1, Pallas kernels, on_device(): pl.pallas_call(prepare_body, out_shape=(taps, taps, pltpu.VMEM((128, 256)...  2.09 us
  transfers between devices with their start and end apart: 6, of which 0 were waited for; matrix products, arithmetic and copies ran while one was open for 0% of the time, Pallas kernels for 32%

profile of v1, /device:TPU:1, one launch (start us, length us, event | category | flops | bytes accessed | tf_op | source)
XLA Modules:
  0.0 91.3 jit_solution(13097480464655559092)
XLA Ops:
  0.6 0.0 copy-start
  0.7 1.4 %open.2.refs_0_.own_b = bf16[2,128,1024]{2,1,0:T(8,128)(2,1)S(1)} custom-call(s32[1]{0:T(128)} %bitcast.1.half.half_b.spot, bf16[64,4,8,256]{3,2,1,0:T(8,128)(2,1)} %bitcast.14), custom_call_target="tpu_custom_call" | custom-call | flops 100000000 | tf_op jit(solution)/shard_map/open/pallas_call | solution.py:136
  2.1 1.3 %open.3.own_a = bf16[2,128,1024]{2,1,0:T(8,128)(2,1)S(1)} custom-call(s32[1]{0:T(128)S(6)} %sub.3.half, bf16[64,4,8,256]{3,2,1,0:T(8,128)(2,1)} %bitcast.15, bf16[2,128,1024]{2,1,0:T(8,128)(2,1)S(1)} %open.2.refs_0_.own_b), custom_call_target="tpu_custom_call" | custom-call | flops 100000000 | tf_op jit(solution)/shard_map/open/pallas_call | solution.py:136
  3.4 1.5 %collective-permute-start = (bf16[2,128,1024]{2,1,0:T(8,128)(2,1)S(1)}, bf16[2,128,1024]{2,1,0:T(8,128)(2,1)}, u32[]{:S(2)}, u32[]{:S(2)}) collective-permute-start(bf16[2,128,1024]{2,1,0:T(8,128)(2,1)S(1)} %open.3.own_a), channel_id=1, source_target_pairs={{0,1},{1,0},{2,3},{3,2},{4,5},{5,4},{6,7},{7,6},{8,9},{9,8},{10,11... | collective-permute-start | bytes 1572872 | tf_op jit(solution)/shard_map/ppermute | solution.py:416
  4.9 3.5 %collective-permute-start.1 = (bf16[2,128,1024]{2,1,0:T(8,128)(2,1)S(1)}, bf16[2,128,1024]{2,1,0:T(8,128)(2,1)}, u32[]{:S(2)}, u32[]{:S(2)}) collective-permute-start(bf16[2,128,1024]{2,1,0:T(8,128)(2,1)S(1)} %open.2.refs_0_.own_b), channel_id=1, source_target_pairs={{1,2},{3,4},{5,6},{7,8},{9,10},{11,12},{13,14},{2,1},{4,3},{6,5},{... | collective-permute-start | bytes 1572872 | tf_op jit(solution)/shard_map/ppermute | solution.py:421
  8.5 0.1 pad_maximum_fusion.mask.refs_0_
  8.5 2.1 %prepare.1 = (bf16[256,1152]{1,0:T(8,128)(2,1)S(1)}, bf16[256,1152]{1,0:T(8,128)(2,1)S(1)}, f32[128,256]{1,0:T(8,128)S(1)}, f32[64,128]{1,0:T(8,128)S(1)}) custom-call(f32[6]{0:T(128)S(1)} %pad_maximum_fusion.mask.refs_0_, bf16[27,64,64]{2,1,0:T(8,128)(2,1)} %weight_in.1, f32[1,64]{1,0:T(1,128)} %bitcast.17), custom_call_target="tpu_custom_call" | custom-call | flops 100000000 | tf_op jit(solution)/shard_map/prepare/pallas_call | solution.py:441
  10.6 0.0 copy-done
  10.6 2.6 %inner.1 = (bf16[3072,1024]{1,0:T(8,128)(2,1)S(1)}, bf16[2304,1024]{1,0:T(8,128)(2,1)S(1)}, f32[6,128,1024]{2,1,0:T(8,128)S(1)}, bf16[4,4,64,128]{3,2,1,0:T(8,12...) custom-call(s32[1]{0:T(128)} %bitcast.1.half.half_b.spot, bf16[2,128,1024]{2,1,0:T(8,128)(2,1)S(1)} %open.3.own_a, ...), custom_call_target="tpu_custom_call" | custom-call | flops 500000000 | tf_op jit(solution)/shard_map/inner/pallas_call | solution.py:97
  13.2 0.0 collective-permute-done.refs_5_
  13.2 4.4 %forward.2 = (bf16[3072,1024]{1,0:T(8,128)(2,1)S(1)}, bf16[2304,1024]{1,0:T(8,128)(2,1)S(1)}, f32[6,128,1024]{2,1,0:T(8,128)S(1)}, bf16[4,4,64,128]{3,2,1,0:T(8,128)(2,1)S(1)}, bf16[3,128,1024]{2,1,0:T(8,128)(2,1)S(1)}) custom-call(s32[1]{0:T(128)S(6)} %sub.3.half, ...), custom_call_target="tpu_custom_call", output_to_operand_aliasing={{0}: (2, {}), {1}: (3, {}), {2}: (4, {}), {3}: (5, {})} | custom-call | flops 400000000 | tf_op jit(solution)/shard_map/forward/pallas_call | solution.py:97
  17.6 0.1 collective-permute-start.2
  17.7 0.0 collective-permute-done.1.refs_5_
  17.7 4.5 %forward.3 = (bf16[3072,1024]{1,0:T(8,128)(2,1)S(1)}, bf16[2304,1024]{1,0:T(8,128)(2,1)S(1)}, f32[6,128,1024]{2,1,0:T(8,128)S(1)}, bf16[4,4,64,128]{3,2,1,0:T(8,128)(2,1)S(1)}, bf16[3,128,1024]{2,1,0:T(8,128)(2,1)S(1)}) custom-call(s32[1]{0:T(128)} %bitcast.1.half.half_b.spot, ...), custom_call_target="tpu_custom_call", output_to_operand_aliasing={{0}: (2, {}), {1}: (3, {}), {2}: (4, {}), {3}: (5, {})} | custom-call | flops 400000000 | tf_op jit(solution)/shard_map/forward/pallas_call | solution.py:97
  22.2 4.0 %collective-permute-start.3 = (bf16[3,128,1024]{2,1,0:T(8,128)(2,1)S(1)}, bf16[3,128,1024]{2,1,0:T(8,128)(2,1)S(1)}, u32[]{:S(2)}, u32[]{:S(2)}) collective-permute-start(bf16[3,128,1024]{2,1,0:T(8,128)(2,1)S(1)} %get-tuple-element.56.own_b), channel_id=1, source_target_pairs={{1,2},{3,4},{5,6},{7,8},{9,10},{11,12},{13,14},{2,1},{4,3},{6,5},{... | collective-permute-start | bytes 2359304 | tf_op jit(solution)/shard_map/ppermute | solution.py:421
  26.2 1.8 %back_inner.1 = (bf16[3072,1024]{1,0:T(8,128)(2,1)S(1)}, bf16[2304,1024]{1,0:T(8,128)(2,1)S(1)}, f32[6,128,1024]{2,1,0:T(8,128)S(1)}, bf16[4,4,64,128]{3,2,1,0:T(8,128)(2,1)S(1)}, f32[128,128]{1,0:T(8,128)S(1)}) custom-call(s32[1]{0:T(128)} %bitcast.1.half.half_b.spot, bf16[3,128,1024]{2,1,0:T(8,128)(2,1)S(1)} %get-tuple-element.51.own_a, ...), custom_call_target="tpu_custom_call" | custom-call | flops 300000000 | tf_op jit(solution)/shard_map/back_inner/pallas_call | solution.py:97
  28.0 0.0 collective-permute-done.2.refs_4_
  28.1 2.6 %back_outer.2 = (bf16[3072,1024]{1,0:T(8,128)(2,1)S(1)}, bf16[2304,1024]{1,0:T(8,128)(2,1)S(1)}, f32[6,128,1024]{2,1,0:T(8,128)S(1)}) custom-call(s32[1]{0:T(128)S(6)} %sub.3.half, f32[6]{0:T(128)S(1)} %pad_maximum_fusion.mask.refs_0_, bf16[3072,1024]{1,0:T(8,128)(2,1)S(1)} %get-tuple-element.59.refs_1_, ...), custom_call_target="tpu_custom_call", output_to_operand_aliasing={{0}: (2, {}), {1}: (3, {}), {2}: (4, {})} | custom-call | flops 300000000 | tf_op jit(solution)/shard_map/back_outer/pallas_call | solution.py:97
  30.6 2.2 %back_last.2.refs_9_.coarse_in = bf16[4,4,64,128]{3,2,1,0:T(8,128)(2,1)S(1)} custom-call(s32[1]{0:T(128)S(6)} %sub.3.half, bf16[2304,1024]{1,0:T(8,128)(2,1)S(1)} %get-tuple-element.65.back0.wide0.refs_2_, f32[6,128,1024]{2,1,0:T(8,128)S(1)} %get-tuple-element.66.middle.refs_3_, ...), custom_call_target="tpu_custom_call", output_to_operand_aliasing={{}: (6, {})} | custom-call | flops 200000000 | tf_op jit(solution)/shard_map/back_last/pallas_call | solution.py:97
  32.8 5.0 %gradient_first.1 = (f32[256,1152]{1,0:T(8,128)S(1)}, f32[128,128]{1,0:T(8,128)S(1)}) custom-call(s32[1]{0:T(128)} %bitcast.1.half.half_b.spot, bf16[3,128,1024]{2,1,0:T(8,128)(2,1)S(1)} %get-tuple-element.51.own_a, bf16[3,128,1024]{2,1,0:T(8,128)(2,1)S(1)} %get-tuple-element.56.own_b, bf16[2304,1024]{1,0:T(8,128)(2,1)S(1)} %get-tuple-element.67.wide1, ...), custom_call_target="tpu_custom_call" | custom-call | flops 500000000 | tf_op jit(solution)/shard_map/gradient_first/pallas_call | solution.py:97
  37.8 0.0 collective-permute-done.3.refs_4_
  37.8 2.3 %back_outer.3 = (bf16[3072,1024]{1,0:T(8,128)(2,1)S(1)}, bf16[2304,1024]{1,0:T(8,128)(2,1)S(1)}, f32[6,128,1024]{2,1,0:T(8,128)S(1)}) custom-call(s32[1]{0:T(128)} %bitcast.1.half.half_b.spot, f32[6]{0:T(128)S(1)} %pad_maximum_fusion.mask.refs_0_, ...), custom_call_target="tpu_custom_call", output_to_operand_aliasing={{0}: (2, {}), {1}: (3, {}), {2}: (4, {})} | custom-call | flops 300000000 | tf_op jit(solution)/shard_map/back_outer/pallas_call | solution.py:97
  40.1 1.1 %gradient_last.1 = (f32[256,1152]{1,0:T(8,128)S(1)}, f32[128,128]{1,0:T(8,128)S(1)}, f32[8,64,128]{2,1,0:T(8,128)S(1)}, f32[8,64,128]{2,1,0:T(8,128)S(1)}) custom-call(s32[1]{0:T(128)} %bitcast.1.half.half_b.spot, bf16[2304,1024]{1,0:T(8,128)(2,1)S(1)} %get-tuple-element.72.back0.wide0, ...), custom_call_target="tpu_custom_call", output_to_operand_aliasing={{0}: (3, {}), {1}: (4, {})} | custom-call | flops 200000000 | tf_op jit(solution)/shard_map/gradient_last/pallas_call | solution.py:97
  41.2 0.1 collective-permute-start.4
  41.3 2.2 %back_last.3 = bf16[4,4,64,128]{3,2,1,0:T(8,128)(2,1)S(1)} custom-call(s32[1]{0:T(128)} %bitcast.1.half.half_b.spot, bf16[2304,1024]{1,0:T(8,128)(2,1)S(1)} %get-tuple-element.72.back0.wide0, f32[6,128,1024]{2,1,0:T(8,128)S(1)} %get-tuple-element.76.middle, f32[4,4,64,128]{3,2,1,0:T(8,128)S(1)} %get-tuple-element.70.average_lam, ...), custom_call_target="tpu_custom_call", output_to_operand_aliasing={{}: (6, {})} | custom-call | flops 200000000 | tf_op jit(solution)/shard_map/back_last/pallas_call | solution.py:97
  43.5 0.0 collective-permute-done.4.received
  43.5 0.1 pack.1
  43.6 16.0 %all_to_all.15.mixed = bf16[8,320,128]{2,1,0:T(8,128)(2,1)S(1)} all-to-all(bf16[8,320,128]{2,1,0:T(8,128)(2,1)S(1)} %get-tuple-element.78), channel_id=1, replica_groups=mesh['tm'=8,'slab'=16] {'tm'}, dimensions={0} | all-to-all | bytes 1310720 | tf_op jit(solution)/shard_map/all_to_all | solution.py:425
  59.6 0.1 meet.1
  59.7 15.4 %all_to_all.16.shared = bf16[8,64,128]{2,1,0:T(8,128)(2,1)S(1)} all-to-all(bf16[8,64,128]{2,1,0:T(8,128)(2,1)S(1)} %get-tuple-element.79), channel_id=1, replica_groups={{0,2,4,6,8,10,12,14},{1,3,5,7,9,11,13,15},{16,18,20,22,24,26,28,30},{17..., dimensions={0} | all-to-all | bytes 262144 | tf_op jit(solution)/shard_map/all_to_all | solution.py:557
  75.2 9.3 %all_to_all.17.joined = bf16[8,192,128]{2,1,0:T(8,128)(2,1)S(1)} all-to-all(bf16[8,192,128]{2,1,0:T(8,128)(2,1)S(1)} %join.1), channel_id=1, replica_groups=mesh['tm'=8,'slab'=16] {'tm'}, dimensions={0} | all-to-all | bytes 786432 | tf_op jit(solution)/shard_map/all_to_all | solution.py:425
  84.5 3.7 %collective-permute-start.5 = (bf16[8,64,128]{2,1,0:T(8,128)(2,1)S(1)}, bf16[8,64,128]{2,1,0:T(8,128)(2,1)S(1)}, u32[]{:S(2)}, u32[]{:S(2)}) collective-permute-start(bf16[8,64,128]{2,1,0:T(8,128)(2,1)S(1)} %slice.4), channel_id=1, source_target_pairs={{0,1},{1,0},{2,3},{3,2},{4,5},{5,4},{6,7},{7,6},{8,9},{9,8},{10,11... | collective-permute-start | bytes 393224 | tf_op jit(solution)/shard_map/ppermute | solution.py:416
  88.2 2.1 %finish.1 = f32[64,4,8,256]{3,2,1,0:T(8,128)} custom-call(f32[64,4,8,256]{3,2,1,0:T(8,128)S(1)} %bitcast.11, f32[4,4,64,128]{3,2,1,0:T(8,128)S(1)} %get-tuple-element.77.average_lam, bf16[8,192,128]{2,1,0:T(8,128)(2,1)S(1)} %all_to_all.17.joined), custom_call_target="tpu_custom_call" | custom-call | flops 300000000 | tf_op jit(solution)/shard_map/finish/pallas_call | solution.py:97
  90.3 0.0 collective-permute-done.5.received
  90.3 1.1 %taps.1 = (f32[27,64,64]{2,1,0:T(8,128)}, f32[1,64]{1,0:T(1,128)}) custom-call(s32[1]{0:T(128)} %bitcast.1.half.half_b.spot, bf16[8,192,128]{2,1,0:T(8,128)(2,1)S(1)} %all_to_all.17.joined, bf16[8,64,128]{2,1,0:T(8,128)(2,1)S(1)} %collective-permute-done.5.received), custom_call_target="tpu_custom_call" | custom-call | flops 100000000 | tf_op jit(solution)/shard_map/taps/pallas_call | solution.py:97
  (3 shorter events, 0.0 us)
Async XLA Ops:
  0.6 10.0 %copy-start = (f32[1,64,4,8,256]{4,3,2,1,0:T(8,128)S(1)}, f32[1,64,4,8,256]{4,3,2,1,0:T(8,128)}, u32[]{:S(2)}) copy-start(f32[1,64,4,8,256]{4,3,2,1,0:T(8,128)} %param.5) | copy-start | bytes 6291460
  3.4 9.8 %collective-permute-start = (bf16[2,128,1024]{2,1,0:T(8,128)(2,1)S(1)}, bf16[2,128,1024]{2,1,0:T(8,128)(2,1)}, u32[]{:S(2)}, u32[]{:S(2)}) collective-permute-start(bf16[2,128,1024]{2,1,0:T(8,128)(2,1)S(1)} %open.3.own_a), channel_id=1, source_target_pairs={{0,1},{1,0},{2,3},{3,2},{4,5},{5,4},{6,7},{7,6},{8,9},{9,8},{10,11... | collective-permute-start | bytes 1572872 | tf_op jit(solution)/shard_map/ppermute | solution.py:416
  4.9 12.8 %collective-permute-start.1 = (bf16[2,128,1024]{2,1,0:T(8,128)(2,1)S(1)}, bf16[2,128,1024]{2,1,0:T(8,128)(2,1)}, u32[]{:S(2)}, u32[]{:S(2)}) collective-permute-start(bf16[2,128,1024]{2,1,0:T(8,128)(2,1)S(1)} %open.2.refs_0_.own_b), channel_id=1, source_target_pairs={{1,2},{3,4},{5,6},{7,8},{9,10},{11,12},{13,14},{2,1},{4,3},{6,5},{... | collective-permute-start | bytes 1572872 | tf_op jit(solution)/shard_map/ppermute | solution.py:421
  17.6 10.4 %collective-permute-start.2 = (bf16[3,128,1024]{2,1,0:T(8,128)(2,1)S(1)}, bf16[3,128,1024]{2,1,0:T(8,128)(2,1)S(1)}, u32[]{:S(2)}, u32[]{:S(2)}) collective-permute-start(bf16[3,128,1024]{2,1,0:T(8,128)(2,1)S(1)} %get-tuple-element.51.own_a), channel_id=1, source_target_pairs={{0,1},{1,0},{2,3},{3,2},{4,5},{5,4},{6,7},{7,6},{8,9},{9,8},{10,11... | collective-permute-start | bytes 2359304 | tf_op jit(solution)/shard_map/ppermute | solution.py:416
  22.2 15.6 %collective-permute-start.3 = (bf16[3,128,1024]{2,1,0:T(8,128)(2,1)S(1)}, bf16[3,128,1024]{2,1,0:T(8,128)(2,1)S(1)}, u32[]{:S(2)}, u32[]{:S(2)}) collective-permute-start(bf16[3,128,1024]{2,1,0:T(8,128)(2,1)S(1)} %get-tuple-element.56.own_b), channel_id=1, source_target_pairs={{1,2},{3,4},{5,6},{7,8},{9,10},{11,12},{13,14},{2,1},{4,3},{6,5},{... | collective-permute-start | bytes 2359304 | tf_op jit(solution)/shard_map/ppermute | solution.py:421
  41.2 2.3 %collective-permute-start.4 = (f32[8,64,128]{2,1,0:T(8,128)S(1)}, f32[8,64,128]{2,1,0:T(8,128)S(1)}, u32[]{:S(2)}, u32[]{:S(2)}) collective-permute-start(f32[8,64,128]{2,1,0:T(8,128)S(1)} %get-tuple-element.75), channel_id=1, source_target_pairs={{0,1},{1,0},{2,3},{3,2},{4,5},{5,4},{6,7},{7,6},{8,9},{9,8},{10,11... | collective-permute-start | bytes 786440 | tf_op jit(solution)/shard_map/ppermute | solution.py:416
  84.5 5.8 %collective-permute-start.5 = (bf16[8,64,128]{2,1,0:T(8,128)(2,1)S(1)}, bf16[8,64,128]{2,1,0:T(8,128)(2,1)S(1)}, u32[]{:S(2)}, u32[]{:S(2)}) collective-permute-start(bf16[8,64,128]{2,1,0:T(8,128)(2,1)S(1)} %slice.4), channel_id=1, source_target_pairs={{0,1},{1,0},{2,3},{3,2},{4,5},{5,4},{6,7},{7,6},{8,9},{9,8},{10,11... | collective-permute-start | bytes 393224 | tf_op jit(solution)/shard_map/ppermute | solution.py:416

commit v2 on v1

--- a/solution.py
+++ b/solution.py
@@ -378,14 +378,21 @@
     offset[...] = jnp.sum(jnp.where(row == col, column, 0.0), axis=0, keepdims=True)
 
 
-def prepare_body(mask, weight_in, bias_in, matrix, flipped, offset, diag, weight, bias, arrived):
+def prepare_body(half, mask, u, weight_in, bias_in, own_b, own_a, matrix, flipped, offset, diag, planes, turn, weight, bias, arrived):
     copies = [
         pltpu.make_async_copy(source, target, arrived.at[index])
-        for index, (source, target) in enumerate(((weight_in, weight), (bias_in, bias)))
+        for index, (source, target) in enumerate(
+            ((u.at[:, pl.ds(2 * half[0], 2)], planes), (weight_in, weight), (bias_in, bias))
+        )
     ]
     for copy in copies:
         copy.start()
-    for copy in copies:
+    copies[0].wait()
+    for place in range(2):
+        to_rows(planes, place, turn)
+        for pair in range(4):
+            own_a[place, :, pair * 256 : pair * 256 + 256] = pair_of(turn, pair).astype(bf16)
+    for copy in copies[1:]:
         copy.wait()
     row = lax.broadcasted_iota(jnp.int32, (64, 64), 0)
     col = lax.broadcasted_iota(jnp.int32, (64, 64), 1)
@@ -435,22 +442,23 @@
     other = 1 - spot
     own_b = opened(spot, u)
     halo_b = across(own_b)
-    own_a = opened(other, u, own_b)
-    halo_a = beside(own_a)
     taps = pltpu.VMEM((256, 1152), bf16)
-    matrix, flipped, offset, diag = pl.pallas_call(
+    own_a, matrix, flipped, offset, diag = pl.pallas_call(
         prepare_body,
-        out_shape=(taps, taps, pltpu.VMEM((128, 256), f32), pltpu.VMEM((64, 128), f32)),
-        in_specs=[pl.BlockSpec(memory_space=pltpu.SMEM)] + [pl.BlockSpec(memory_space=pl.ANY)] * 2,
+        out_shape=(field(2, bf16), taps, taps, pltpu.VMEM((128, 256), f32), pltpu.VMEM((64, 128), f32)),
+        in_specs=[pl.BlockSpec(memory_space=pltpu.SMEM)] * 2 + [pl.BlockSpec(memory_space=pl.ANY)] * 4,
         scratch_shapes=[
+            pltpu.VMEM((64, 2, 8, 256), bf16),
+            TURN,
             pltpu.VMEM(weight.shape, bf16),
             pltpu.VMEM((1, 64), f32),
-            pltpu.SemaphoreType.DMA((2,)),
+            pltpu.SemaphoreType.DMA((3,)),
         ],
         compiler_params=pltpu.CompilerParams(vmem_limit_bytes=8 * 2**20),
         cost_estimate=pl.CostEstimate(flops=10**8, bytes_accessed=0, transcendentals=0),
         name="prepare",
-    )(mask, *(pltpu.with_memory_space_constraint(v, pltpu.HBM) for v in (weight, bias[None])))
+    )(other, mask, *(pltpu.with_memory_space_constraint(v, pltpu.HBM) for v in (u, weight, bias[None])), own_b)
+    halo_a = beside(own_a)
     matrix, flipped, offset, diag = (near(v) for v in (matrix, flipped, offset, diag))
     coarse_shape = pltpu.VMEM((4, 4, 64, 128), bf16)
     average_shape = (4, 4, 64, 128)

time: 91.7 us -> 91.7 us (level)
  Pallas kernels: 36.8 us -> 34.7 us
  blocking collectives: 40.7 us -> 42.8 us
    all_to_all x1, blocking collectives: 15.4 us -> 17.6 us  [on_device(): lax.all_to_all(shared, 'slab', 0, 0, tiled=True, axis_index_groups=same_c...]
    pallas_call x2 -> x1, Pallas kernels: 2.73 us -> 1.44 us  [opened(): pl.pallas_call(open_body, out_shape=field(2, bf16), in_specs=[pl.BlockSpe...]
    pallas_call x15, Pallas kernels: 32 us -> 30.9 us  [run(): pl.pallas_call(body, out_shape=outs, in_specs=in_specs, scratch_shapes=li...]
  transfers between devices with their start and end apart: 6 -> 6, of which waited for: 0 -> 1; matrix products, arithmetic and copies ran while one was open for 0% -> 0% of each run, Pallas kernels for 32% -> 29%
where the time goes in v2:
time: 91.7 us; the launch traced here: 91.5 us
  blocking collectives  42.8 us (47%)
  Pallas kernels  34.7 us (38%)
  starting transfers between devices  12.6 us (14%)
    pallas_call x15, Pallas kernels, run(): pl.pallas_call(body, out_shape=outs, in_specs=in_specs, scratch_shapes=li...  30.9 us
    all_to_all x2, blocking collectives, exchanged(): return lax.all_to_all(value, axes, 0, 0, tiled=True)  25.2 us
    all_to_all x1, blocking collectives, on_device(): lax.all_to_all(shared, 'slab', 0, 0, tiled=True, axis_index_groups=same_c...  17.6 us
    ppermute x2, starting transfers between devices, across(): return lax.ppermute(value, 'slab', up + [(j, i) for i, j in up])  7.13 us
    ppermute x4, starting transfers between devices, beside(): lax.ppermute(value, 'slab', [(i, i ^ 1) for i in range(lax.axis_size('sla...  5.42 us
    pallas_call x1, Pallas kernels, on_device(): pl.pallas_call(prepare_body, out_shape=(field(2, bf16), taps, taps, pltpu...  2.37 us
  transfers between devices with their start and end apart: 6, of which 1 were waited for; matrix products, arithmetic and copies ran while one was open for 0% of the time, Pallas kernels for 29%

profile of v2, /device:TPU:1, one launch (start us, length us, event | category | flops | bytes accessed | tf_op | source)
XLA Modules:
  0.0 91.5 jit_solution(4040124622296301664)
XLA Ops:
  0.6 0.0 copy-start
  0.7 1.4 %open.1.own_b = bf16[2,128,1024]{2,1,0:T(8,128)(2,1)S(1)} custom-call(s32[1]{0:T(128)} %bitcast.1.half.half_b.spot, bf16[64,4,8,256]{3,2,1,0:T(8,128)(2,1)} %bitcast.14), custom_call_target="tpu_custom_call" | custom-call | flops 100000000 | tf_op jit(solution)/shard_map/open/pallas_call | solution.py:136
  2.1 0.1 pad_maximum_fusion.mask.refs_0_
  2.2 2.4 %prepare.1 = (bf16[2,128,1024]{2,1,0:T(8,128)(2,1)S(1)}, bf16[256,1152]{1,0:T(8,128)(2,1)S(1)}, bf16[256,1152]{1,0:T(8,128)(2,1)S(1)}, f32[128,256]{1,0:T(8,128)S(1)}, f32[64,128]{1,0:T(8,128)S(1)}) custom-call(s32[1]{0:T(128)S(6)} %sub.3.half, f32[6]{0:T(128)S(1)} %pad_maximum_fusion.mask.refs_0_, bf16[64,4,8,256]{3,2,1,0:T(8,128)(2,1)} %bitcast.15, ...), custom_call_target="tpu_custom_call" | custom-call | flops 100000000 | tf_op jit(solution)/shard_map/prepare/pallas_call | solution.py:446
  4.6 1.5 %collective-permute-start = (bf16[2,128,1024]{2,1,0:T(8,128)(2,1)S(1)}, bf16[2,128,1024]{2,1,0:T(8,128)(2,1)S(1)}, u32[]{:S(2)}, u32[]{:S(2)}) collective-permute-start(bf16[2,128,1024]{2,1,0:T(8,128)(2,1)S(1)} %get-tuple-element.44.own_a), channel_id=1, source_target_pairs={{0,1},{1,0},{2,3},{3,2},{4,5},{5,4},{6,7},{7,6},{8,9},{9,8},{10,11... | collective-permute-start | bytes 1572872 | tf_op jit(solution)/shard_map/ppermute | solution.py:423
  6.1 3.5 %collective-permute-start.1 = (bf16[2,128,1024]{2,1,0:T(8,128)(2,1)S(1)}, bf16[2,128,1024]{2,1,0:T(8,128)(2,1)S(1)}, u32[]{:S(2)}, u32[]{:S(2)}) collective-permute-start(bf16[2,128,1024]{2,1,0:T(8,128)(2,1)S(1)} %open.1.own_b), channel_id=1, source_target_pairs={{1,2},{3,4},{5,6},{7,8},{9,10},{11,12},{13,14},{2,1},{4,3},{6,5},{... | collective-permute-start | bytes 1572872 | tf_op jit(solution)/shard_map/ppermute | solution.py:428
  9.6 0.0 copy-done
  9.6 2.6 %inner.1 = (bf16[3072,1024]{1,0:T(8,128)(2,1)S(1)}, bf16[2304,1024]{1,0:T(8,128)(2,1)S(1)}, f32[6,128,1024]{2,1,0:T(8,128)S(1)}, bf16[4,4,64,128]{3,2,1,0:T(8,12...) custom-call(s32[1]{0:T(128)} %bitcast.1.half.half_b.spot, ...), custom_call_target="tpu_custom_call" | custom-call | flops 500000000 | tf_op jit(solution)/shard_map/inner/pallas_call | solution.py:97
  12.2 0.0 collective-permute-done.refs_5_
  12.2 3.9 %forward.2 = (bf16[3072,1024]{1,0:T(8,128)(2,1)S(1)}, bf16[2304,1024]{1,0:T(8,128)(2,1)S(1)}, f32[6,128,1024]{2,1,0:T(8,128)S(1)}, bf16[4,4,64,128]{3,2,1,0:T(8,128)(2,1)S(1)}, bf16[3,128,1024]{2,1,0:T(8,128)(2,1)S(1)}) custom-call(s32[1]{0:T(128)S(6)} %sub.3.half, ...), custom_call_target="tpu_custom_call", output_to_operand_aliasing={{0}: (2, {}), {1}: (3, {}), {2}: (4, {}), {3}: (5, {})} | custom-call | flops 400000000 | tf_op jit(solution)/shard_map/forward/pallas_call | solution.py:97
  16.1 0.1 collective-permute-start.2
  16.2 0.4 collective-permute-done.1.refs_5_
  16.6 4.0 %forward.3 = (bf16[3072,1024]{1,0:T(8,128)(2,1)S(1)}, bf16[2304,1024]{1,0:T(8,128)(2,1)S(1)}, f32[6,128,1024]{2,1,0:T(8,128)S(1)}, bf16[4,4,64,128]{3,2,1,0:T(8,128)(2,1)S(1)}, bf16[3,128,1024]{2,1,0:T(8,128)(2,1)S(1)}) custom-call(s32[1]{0:T(128)} %bitcast.1.half.half_b.spot, ...), custom_call_target="tpu_custom_call", output_to_operand_aliasing={{0}: (2, {}), {1}: (3, {}), {2}: (4, {}), {3}: (5, {})} | custom-call | flops 400000000 | tf_op jit(solution)/shard_map/forward/pallas_call | solution.py:97
  20.5 3.6 %collective-permute-start.3 = (bf16[3,128,1024]{2,1,0:T(8,128)(2,1)S(1)}, bf16[3,128,1024]{2,1,0:T(8,128)(2,1)S(1)}, u32[]{:S(2)}, u32[]{:S(2)}) collective-permute-start(bf16[3,128,1024]{2,1,0:T(8,128)(2,1)S(1)} %get-tuple-element.58.own_b), channel_id=1, source_target_pairs={{1,2},{3,4},{5,6},{7,8},{9,10},{11,12},{13,14},{2,1},{4,3},{6,5},{... | collective-permute-start | bytes 2359304 | tf_op jit(solution)/shard_map/ppermute | solution.py:428
  24.2 1.8 %back_inner.1 = (bf16[3072,1024]{1,0:T(8,128)(2,1)S(1)}, bf16[2304,1024]{1,0:T(8,128)(2,1)S(1)}, f32[6,128,1024]{2,1,0:T(8,128)S(1)}, bf16[4,4,64,128]{3,2,1,0:T(8,128)(2,1)S(1)}, f32[128,128]{1,0:T(8,128)S(1)}) custom-call(s32[1]{0:T(128)} %bitcast.1.half.half_b.spot, bf16[3,128,1024]{2,1,0:T(8,128)(2,1)S(1)} %get-tuple-element.53.own_a, ...), custom_call_target="tpu_custom_call" | custom-call | flops 300000000 | tf_op jit(solution)/shard_map/back_inner/pallas_call | solution.py:97
  26.0 0.0 collective-permute-done.2.refs_4_
  26.0 2.6 %back_outer.2 = (bf16[3072,1024]{1,0:T(8,128)(2,1)S(1)}, bf16[2304,1024]{1,0:T(8,128)(2,1)S(1)}, f32[6,128,1024]{2,1,0:T(8,128)S(1)}) custom-call(s32[1]{0:T(128)S(6)} %sub.3.half, f32[6]{0:T(128)S(1)} %pad_maximum_fusion.mask.refs_0_, bf16[3072,1024]{1,0:T(8,128)(2,1)S(1)} %get-tuple-element.61.refs_1_, ...), custom_call_target="tpu_custom_call", output_to_operand_aliasing={{0}: (2, {}), {1}: (3, {}), {2}: (4, {})} | custom-call | flops 300000000 | tf_op jit(solution)/shard_map/back_outer/pallas_call | solution.py:97
  28.6 2.2 %back_last.2.refs_9_.coarse_in = bf16[4,4,64,128]{3,2,1,0:T(8,128)(2,1)S(1)} custom-call(s32[1]{0:T(128)S(6)} %sub.3.half, bf16[2304,1024]{1,0:T(8,128)(2,1)S(1)} %get-tuple-element.67.back0.wide0.refs_2_, f32[6,128,1024]{2,1,0:T(8,128)S(1)} %get-tuple-element.68.middle.refs_3_, ...), custom_call_target="tpu_custom_call", output_to_operand_aliasing={{}: (6, {})} | custom-call | flops 200000000 | tf_op jit(solution)/shard_map/back_last/pallas_call | solution.py:97
  30.8 5.0 %gradient_first.1 = (f32[256,1152]{1,0:T(8,128)S(1)}, f32[128,128]{1,0:T(8,128)S(1)}) custom-call(s32[1]{0:T(128)} %bitcast.1.half.half_b.spot, bf16[3,128,1024]{2,1,0:T(8,128)(2,1)S(1)} %get-tuple-element.53.own_a, bf16[3,128,1024]{2,1,0:T(8,128)(2,1)S(1)} %get-tuple-element.58.own_b, bf16[2304,1024]{1,0:T(8,128)(2,1)S(1)} %get-tuple-element.69.wide1, ...), custom_call_target="tpu_custom_call" | custom-call | flops 500000000 | tf_op jit(solution)/shard_map/gradient_first/pallas_call | solution.py:97
  35.8 0.0 collective-permute-done.3.refs_4_
  35.8 2.3 %back_outer.3 = (bf16[3072,1024]{1,0:T(8,128)(2,1)S(1)}, bf16[2304,1024]{1,0:T(8,128)(2,1)S(1)}, f32[6,128,1024]{2,1,0:T(8,128)S(1)}) custom-call(s32[1]{0:T(128)} %bitcast.1.half.half_b.spot, f32[6]{0:T(128)S(1)} %pad_maximum_fusion.mask.refs_0_, ...), custom_call_target="tpu_custom_call", output_to_operand_aliasing={{0}: (2, {}), {1}: (3, {}), {2}: (4, {})} | custom-call | flops 300000000 | tf_op jit(solution)/shard_map/back_outer/pallas_call | solution.py:97
  38.1 1.1 %gradient_last.1 = (f32[256,1152]{1,0:T(8,128)S(1)}, f32[128,128]{1,0:T(8,128)S(1)}, f32[8,64,128]{2,1,0:T(8,128)S(1)}, f32[8,64,128]{2,1,0:T(8,128)S(1)}) custom-call(s32[1]{0:T(128)} %bitcast.1.half.half_b.spot, bf16[2304,1024]{1,0:T(8,128)(2,1)S(1)} %get-tuple-element.74.back0.wide0, ...), custom_call_target="tpu_custom_call", output_to_operand_aliasing={{0}: (3, {}), {1}: (4, {})} | custom-call | flops 200000000 | tf_op jit(solution)/shard_map/gradient_last/pallas_call | solution.py:97
  39.2 0.1 collective-permute-start.4
  39.2 2.2 %back_last.3 = bf16[4,4,64,128]{3,2,1,0:T(8,128)(2,1)S(1)} custom-call(s32[1]{0:T(128)} %bitcast.1.half.half_b.spot, bf16[2304,1024]{1,0:T(8,128)(2,1)S(1)} %get-tuple-element.74.back0.wide0, f32[6,128,1024]{2,1,0:T(8,128)S(1)} %get-tuple-element.78.middle, f32[4,4,64,128]{3,2,1,0:T(8,128)S(1)} %get-tuple-element.72.average_lam, ...), custom_call_target="tpu_custom_call", output_to_operand_aliasing={{}: (6, {})} | custom-call | flops 200000000 | tf_op jit(solution)/shard_map/back_last/pallas_call | solution.py:97
  41.5 0.0 collective-permute-done.4.received
  41.5 0.1 pack.1
  41.6 16.0 %all_to_all.15.mixed = bf16[8,320,128]{2,1,0:T(8,128)(2,1)S(1)} all-to-all(bf16[8,320,128]{2,1,0:T(8,128)(2,1)S(1)} %get-tuple-element.80), channel_id=1, replica_groups=mesh['tm'=8,'slab'=16] {'tm'}, dimensions={0} | all-to-all | bytes 1310720 | tf_op jit(solution)/shard_map/all_to_all | solution.py:432
  57.5 0.1 meet.1
  57.7 17.6 %all_to_all.16.shared = bf16[8,64,128]{2,1,0:T(8,128)(2,1)S(1)} all-to-all(bf16[8,64,128]{2,1,0:T(8,128)(2,1)S(1)} %get-tuple-element.81), channel_id=1, replica_groups={{0,2,4,6,8,10,12,14},{1,3,5,7,9,11,13,15},{16,18,20,22,24,26,28,30},{17..., dimensions={0} | all-to-all | bytes 262144 | tf_op jit(solution)/shard_map/all_to_all | solution.py:565
  75.3 9.3 %all_to_all.17.joined = bf16[8,192,128]{2,1,0:T(8,128)(2,1)S(1)} all-to-all(bf16[8,192,128]{2,1,0:T(8,128)(2,1)S(1)} %join.1), channel_id=1, replica_groups=mesh['tm'=8,'slab'=16] {'tm'}, dimensions={0} | all-to-all | bytes 786432 | tf_op jit(solution)/shard_map/all_to_all | solution.py:432
  84.6 3.7 %collective-permute-start.5 = (bf16[8,64,128]{2,1,0:T(8,128)(2,1)S(1)}, bf16[8,64,128]{2,1,0:T(8,128)(2,1)S(1)}, u32[]{:S(2)}, u32[]{:S(2)}) collective-permute-start(bf16[8,64,128]{2,1,0:T(8,128)(2,1)S(1)} %slice.4), channel_id=1, source_target_pairs={{0,1},{1,0},{2,3},{3,2},{4,5},{5,4},{6,7},{7,6},{8,9},{9,8},{10,11... | collective-permute-start | bytes 393224 | tf_op jit(solution)/shard_map/ppermute | solution.py:423
  88.3 2.1 %finish.1 = f32[64,4,8,256]{3,2,1,0:T(8,128)} custom-call(f32[64,4,8,256]{3,2,1,0:T(8,128)S(1)} %bitcast.11, f32[4,4,64,128]{3,2,1,0:T(8,128)S(1)} %get-tuple-element.79.average_lam, bf16[8,192,128]{2,1,0:T(8,128)(2,1)S(1)} %all_to_all.17.joined), custom_call_target="tpu_custom_call" | custom-call | flops 300000000 | tf_op jit(solution)/shard_map/finish/pallas_call | solution.py:97
  90.4 0.0 collective-permute-done.5.received
  90.4 1.1 %taps.1 = (f32[27,64,64]{2,1,0:T(8,128)}, f32[1,64]{1,0:T(1,128)}) custom-call(s32[1]{0:T(128)} %bitcast.1.half.half_b.spot, bf16[8,192,128]{2,1,0:T(8,128)(2,1)S(1)} %all_to_all.17.joined, bf16[8,64,128]{2,1,0:T(8,128)(2,1)S(1)} %collective-permute-done.5.received), custom_call_target="tpu_custom_call" | custom-call | flops 100000000 | tf_op jit(solution)/shard_map/taps/pallas_call | solution.py:97
  (3 shorter events, 0.0 us)
Async XLA Ops:
  0.6 9.0 %copy-start = (f32[1,64,4,8,256]{4,3,2,1,0:T(8,128)S(1)}, f32[1,64,4,8,256]{4,3,2,1,0:T(8,128)}, u32[]{:S(2)}) copy-start(f32[1,64,4,8,256]{4,3,2,1,0:T(8,128)} %param.5) | copy-start | bytes 6291460
  4.6 7.6 %collective-permute-start = (bf16[2,128,1024]{2,1,0:T(8,128)(2,1)S(1)}, bf16[2,128,1024]{2,1,0:T(8,128)(2,1)S(1)}, u32[]{:S(2)}, u32[]{:S(2)}) collective-permute-start(bf16[2,128,1024]{2,1,0:T(8,128)(2,1)S(1)} %get-tuple-element.44.own_a), channel_id=1, source_target_pairs={{0,1},{1,0},{2,3},{3,2},{4,5},{5,4},{6,7},{7,6},{8,9},{9,8},{10,11... | collective-permute-start | bytes 1572872 | tf_op jit(solution)/shard_map/ppermute | solution.py:423
  6.1 10.5 %collective-permute-start.1 = (bf16[2,128,1024]{2,1,0:T(8,128)(2,1)S(1)}, bf16[2,128,1024]{2,1,0:T(8,128)(2,1)S(1)}, u32[]{:S(2)}, u32[]{:S(2)}) collective-permute-start(bf16[2,128,1024]{2,1,0:T(8,128)(2,1)S(1)} %open.1.own_b), channel_id=1, source_target_pairs={{1,2},{3,4},{5,6},{7,8},{9,10},{11,12},{13,14},{2,1},{4,3},{6,5},{... | collective-permute-start | bytes 1572872 | tf_op jit(solution)/shard_map/ppermute | solution.py:428
  16.1 9.9 %collective-permute-start.2 = (bf16[3,128,1024]{2,1,0:T(8,128)(2,1)S(1)}, bf16[3,128,1024]{2,1,0:T(8,128)(2,1)S(1)}, u32[]{:S(2)}, u32[]{:S(2)}) collective-permute-start(bf16[3,128,1024]{2,1,0:T(8,128)(2,1)S(1)} %get-tuple-element.53.own_a), channel_id=1, source_target_pairs={{0,1},{1,0},{2,3},{3,2},{4,5},{5,4},{6,7},{7,6},{8,9},{9,8},{10,11... | collective-permute-start | bytes 2359304 | tf_op jit(solution)/shard_map/ppermute | solution.py:423
  20.5 15.2 %collective-permute-start.3 = (bf16[3,128,1024]{2,1,0:T(8,128)(2,1)S(1)}, bf16[3,128,1024]{2,1,0:T(8,128)(2,1)S(1)}, u32[]{:S(2)}, u32[]{:S(2)}) collective-permute-start(bf16[3,128,1024]{2,1,0:T(8,128)(2,1)S(1)} %get-tuple-element.58.own_b), channel_id=1, source_target_pairs={{1,2},{3,4},{5,6},{7,8},{9,10},{11,12},{13,14},{2,1},{4,3},{6,5},{... | collective-permute-start | bytes 2359304 | tf_op jit(solution)/shard_map/ppermute | solution.py:428
  39.2 2.3 %collective-permute-start.4 = (f32[8,64,128]{2,1,0:T(8,128)S(1)}, f32[8,64,128]{2,1,0:T(8,128)S(1)}, u32[]{:S(2)}, u32[]{:S(2)}) collective-permute-start(f32[8,64,128]{2,1,0:T(8,128)S(1)} %get-tuple-element.77), channel_id=1, source_target_pairs={{0,1},{1,0},{2,3},{3,2},{4,5},{5,4},{6,7},{7,6},{8,9},{9,8},{10,11... | collective-permute-start | bytes 786440 | tf_op jit(solution)/shard_map/ppermute | solution.py:423
  84.6 5.8 %collective-permute-start.5 = (bf16[8,64,128]{2,1,0:T(8,128)(2,1)S(1)}, bf16[8,64,128]{2,1,0:T(8,128)(2,1)S(1)}, u32[]{:S(2)}, u32[]{:S(2)}) collective-permute-start(bf16[8,64,128]{2,1,0:T(8,128)(2,1)S(1)} %slice.4), channel_id=1, source_target_pairs={{0,1},{1,0},{2,3},{3,2},{4,5},{5,4},{6,7},{7,6},{8,9},{9,8},{10,11... | collective-permute-start | bytes 393224 | tf_op jit(solution)/shard_map/ppermute | solution.py:423
